TPU v7x, 32 devices: a whole 2x2x4 slice. The times are simulated.
32 devices in a mesh: groups: 2 (over x), fsdp: 16 (over z, y, core).
Axes of the slice: x: 2, y: 2, z: 4, core: 2. Of those that a mesh axis runs over, the one named last changes fastest.
Arguments:
- tokens: bfloat16 [8192, 8192], P(('groups', 'fsdp')), parts along dimension 0, may hold values from -6 to 6
- token_job_index: int32 [8192, 1], P(('groups', 'fsdp')), parts along dimension 0, may hold values from 0 to 63; in each aligned block of 256 rows (0 to 255, 256 to 511, ...) at most 5 rows name the same one
- cotangent: bfloat16 [8192, 1024], P(('groups', 'fsdp')), parts along dimension 0, may hold values from -0.375 to 0.375
- frozen_value_weight: bfloat16 [8192, 1024], P('fsdp'), may hold values from -0.0625 to 0.0625
- frozen_value_bias: bfloat16 [1024], replicated, may hold values from -3 to 3
- down_factor_weight: bfloat16 [128, 8192, 128], P(('groups', 'fsdp')), parts along dimension 0, may hold values from -0.0625 to 0.0625
- up_factor_weight: bfloat16 [128, 128, 1024], P(('groups', 'fsdp')), parts along dimension 0, may hold values from -0.5 to 0.5
Outputs:
- output: bfloat16 [8192, 1024], P(('groups', 'fsdp')), parts along dimension 0
- down_factor_gradient: bfloat16 [128, 8192, 128], P(('groups', 'fsdp')), parts along dimension 0
- up_factor_gradient: bfloat16 [128, 128, 1024], P(('groups', 'fsdp')), parts along dimension 0
There are 2 independent parts, one for each index of `groups`. A program takes and returns all parts, laid end to end along the dimension named above; an argument that names none is the same for every part. Nothing has to cross between parts.
Inputs may be any that keep to these rules, and one draw needn't show every extreme that they name: `token_job_index`: among the 256 tokens of one device no job appears more than 5 times; some job reaches 5 on some device.
All inputs are finite; a program needn't handle non-finite values.
Results may differ from a plain program's by a relative error of at most 0.0051.
Values may be sent and summed in bfloat16 or wider, within the bound.
A program may use at most 128 MiB of HBM per device.

v0:
```python
import jax
import jax.numpy as jnp
from jax import lax
from jax.sharding import PartitionSpec as P

ADAPTER_JOBS = 64
JOB_TOKEN_LIMIT = 5


def body(
    tokens,
    token_job_index,
    cotangent,
    frozen_value_weight,
    frozen_value_bias,
    down_factor_weight,
    up_factor_weight,
):
    row_count = tokens.shape[0]
    device_job_index = down_factor_weight.shape[0]
    devices = lax.axis_size("fsdp")
    job_list = token_job_index[:, 0]
    one_hot = (job_list[:, None] == jnp.arange(ADAPTER_JOBS, dtype=jnp.int32)[None, :]).astype(
        jnp.int32
    )
    earlier = jnp.cumsum(one_hot, axis=0) - one_hot
    slot_in = jnp.sum(earlier * one_hot, axis=1)
    target = job_list * JOB_TOKEN_LIMIT + slot_in
    matches = (
        target[None, :] == jnp.arange(ADAPTER_JOBS * JOB_TOKEN_LIMIT, dtype=jnp.int32)[:, None]
    )
    filled = jnp.any(matches, axis=1)
    source = jnp.sum(
        matches.astype(jnp.int32) * jnp.arange(row_count, dtype=jnp.int32)[None, :], axis=1
    )
    sent_rows = jnp.where(filled[:, None], tokens[source], jnp.zeros((), tokens.dtype))
    sent_rows = sent_rows.reshape(devices, device_job_index, JOB_TOKEN_LIMIT, tokens.shape[1])
    sent_grads = jnp.where(filled[:, None], cotangent[source], jnp.zeros((), cotangent.dtype))
    sent_grads = sent_grads.reshape(devices, device_job_index, JOB_TOKEN_LIMIT, cotangent.shape[1])
    local_token_rows = lax.all_to_all(sent_rows, "fsdp", split_axis=0, concat_axis=2, tiled=True)
    local_token_rows = local_token_rows[0]
    hidden_input = jnp.einsum(
        "ypk,ykv->ypv", local_token_rows, down_factor_weight, preferred_element_type=jnp.float32
    ).astype(jnp.bfloat16)
    adapter_update = jnp.einsum(
        "ewg,egf->ewf", hidden_input, up_factor_weight, preferred_element_type=jnp.float32
    ).astype(jnp.bfloat16)
    returned_output = lax.all_to_all(
        adapter_update[None], "fsdp", split_axis=2, concat_axis=0, tiled=True
    )
    returned_output = returned_output.reshape(
        ADAPTER_JOBS * JOB_TOKEN_LIMIT, adapter_update.shape[2]
    )
    delta_tokens = returned_output[target]
    local_gradient_rows = lax.all_to_all(
        sent_grads, "fsdp", split_axis=0, concat_axis=2, tiled=True
    )
    local_gradient_rows = local_gradient_rows[0]
    rank_space_gradient = jnp.einsum(
        "buz,bhz->buh", local_gradient_rows, up_factor_weight, preferred_element_type=jnp.float32
    ).astype(jnp.bfloat16)
    up_factor_gradient = jnp.einsum(
        "jtr,jtk->jrk", hidden_input, local_gradient_rows, preferred_element_type=jnp.float32
    ).astype(jnp.bfloat16)
    down_factor_gradient = jnp.einsum(
        "jtd,jtr->jdr", local_token_rows, rank_space_gradient, preferred_element_type=jnp.float32
    ).astype(jnp.bfloat16)
    base_out = jnp.dot(
        tokens,
        lax.all_gather(frozen_value_weight, "fsdp", axis=0, tiled=True),
        preferred_element_type=jnp.float32,
    )
    output = (
        base_out + frozen_value_bias.astype(jnp.float32)[None, :] + delta_tokens.astype(jnp.float32)
    ).astype(jnp.bfloat16)
    return (output, down_factor_gradient, up_factor_gradient)


def solution(mesh):
    return jax.shard_map(
        body,
        mesh=mesh,
        in_specs=(
            P(("groups", "fsdp"), None),
            P(("groups", "fsdp"), None),
            P(("groups", "fsdp"), None),
            P("fsdp", None),
            P(),
            P(("groups", "fsdp"), None, None),
            P(("groups", "fsdp"), None, None),
        ),
        out_specs=(
            P(("groups", "fsdp"), None),
            P(("groups", "fsdp"), None, None),
            P(("groups", "fsdp"), None, None),
        ),
        check_vma=False,
    )
```

profile of v0, /device:TPU:0, one launch (start us, length us, event | category | flops | bytes accessed | tf_op | source)
XLA Modules:
  0.0 309.6 jit_solution(9964029832975064392)
XLA Ops:
  7.2 0.7 all-gather.2.cloned.1.call-update
  7.9 0.7 fusion.16
  8.6 0.6 reduce-window.6
  9.2 0.2 slice_reduce_fusion
  9.4 0.8 fusion.15
  10.2 0.7 multiply_add_fusion
  10.9 0.1 select_reduce_fusion
  11.1 17.2 %gather_fusion = bf16[320,8192]{1,0:T(8,128)(2,1)} fusion(bf16[256,8192]{1,0:T(8,128)(2,1)} %param.7, s32[1024]{0:T(1024)S(1)} %pad_clamp_fusion.1), kind=kCustom, calls=%fused_computation | custom fusion | bytes 10487040 | tf_op jit(solution)/shard_map/gather | solution.py:36
  28.3 8.5 %gather.14 = bf16[16,4,5,8192]{3,2,1,0:T(8,128)(2,1)} reshape(bf16[320,8192]{1,0:T(8,128)(2,1)} %gather_fusion) | data formatting | bytes 10485760 | tf_op jit(solution)/shard_map/gather | solution.py:36
  36.8 0.1 fusion.12
  37.0 0.2 broadcast_in_dim.39
  37.1 7.7 %broadcast_select_fusion = bf16[16,4,5,8192]{3,2,1,0:T(8,128)(2,1)} fusion(bf16[16,4,5,8192]{3,2,1,0:T(8,128)(2,1)} %gather.14, pred[16,4,5]{2,1,0:T(4,128)(4,1)S(1)} %broadcast_in_dim.39), kind=kLoop, calls=%fused_computation.4 | loop fusion | flops 2621440 | bytes 10486080 | tf_op jit(solution)/shard_map/jit(_where)/select_n | solution.py:36
  44.8 10.8 %copy.31 = bf16[16,4,5,8192]{3,1,2,0:T(4,128)(2,1)} copy(bf16[16,4,5,8192]{3,2,1,0:T(8,128)(2,1)} %broadcast_select_fusion) | data formatting | bytes 10485760 | tf_op jit(solution)/shard_map/jit(_where)/select_n | solution.py:36
  55.6 7.5 %all-to-all-start = ((bf16[16,4,5,8192]{3,1,2,0:T(4,128)(2,1)}), bf16[16,4,5,8192]{3,1,2,0:T(4,128)(2,1)}, u32[]{:S(2)}, u32[]{:S(2)}) async-start(bf16[16,4,5,8192]{3,1,2,0:T(4,128)(2,1)} %copy.31), calls=%async_computation | async-start | bytes 10485760 | tf_op jit(solution)/shard_map/all_to_all | solution.py:40
  63.2 2.1 gather_fusion.2
  65.3 0.3 gather.17
  65.6 0.2 broadcast_select_fusion.1
  65.7 1.5 copy.35
  67.2 159.7 %all-to-all-done = bf16[16,4,5,8192]{3,1,2,0:T(4,128)(2,1)} async-done(((bf16[16,4,5,8192]{3,1,2,0:T(4,128)(2,1)}), bf16[16,4,5,8192]{3,1,2,0:T(4,128)(2,1)}, u32[]{:S(2)}, u32[]{:S(2)}) %all-to-all-start) | async-done | bytes 5242912 | tf_op jit(solution)/shard_map/all_to_all | solution.py:40
  226.9 23.7 %all-to-all-start.2 = ((bf16[16,4,5,1024]{3,1,2,0:T(4,128)(2,1)}), bf16[16,4,5,1024]{3,1,2,0:T(4,128)(2,1)S(1)}, u32[]{:S(2)}, u32[]{:S(2)}) async-start(bf16[16,4,5,1024]{3,1,2,0:T(4,128)(2,1)} %copy.35), calls=%async_computation.2 | async-start | bytes 1310720 | tf_op jit(solution)/shard_map/all_to_all | solution.py:55
  250.6 11.1 %fusion.6 = bf16[4,80,128]{2,1,0:T(8,128)(2,1)S(1)} fusion(bf16[4,8192,128]{2,1,0:T(8,128)(2,1)} %param.12, bf16[4,80,8192]{2,0,1:T(4,128)(2,1)} %bitcast.5), kind=kOutput, calls=%fused_computation.14 | convolution fusion | flops 671129600 | bytes 13713408 | tf_op jit(solution)/shard_map/ypk,ykv->ypv/dot_general | solution.py:42
  261.7 0.3 fusion.5
  262.0 1.4 copy.33
  263.4 3.8 %all-to-all-done.2 = bf16[16,4,5,1024]{3,1,2,0:T(4,128)(2,1)S(1)} async-done(((bf16[16,4,5,1024]{3,1,2,0:T(4,128)(2,1)}), bf16[16,4,5,1024]{3,1,2,0:T(4,128)(2,1)S(1)}, u32[]{:S(2)}, u32[]{:S(2)}) %all-to-all-start.2) | async-done | bytes 655392 | tf_op jit(solution)/shard_map/all_to_all | solution.py:55
  267.2 4.8 %all-to-all-start.1 = ((bf16[1,4,80,1024]{3,1,0,2:T(4,128)(2,1)}), bf16[1,4,80,1024]{3,1,0,2:T(4,128)(2,1)S(1)}, u32[]{:S(2)}, u32[]{:S(2)}) async-start(bf16[1,4,80,1024]{3,1,0,2:T(4,128)(2,1)} %copy.33), calls=%async_computation.1 | async-start | bytes 1310720 | tf_op jit(solution)/shard_map/all_to_all | solution.py:48
  272.1 1.6 convolution_convert_fusion.1
  273.6 11.9 %convolution_convert_fusion = bf16[4,8192,128]{2,1,0:T(8,128)(2,1)} fusion(bf16[4,80,8192]{2,0,1:T(4,128)(2,1)} %bitcast.5, bf16[4,128,1024]{2,1,0:T(8,128)(2,1)S(1)} %copy-done, bf16[4,80,1024]{2,0,1:T(4,128)(2,1)S(1)} %bitcast.48), kind=kOutput, calls=%fused_computation.3 | convolution fusion | flops 759209984 | bytes 15335424 | tf_op jit(solution)/shard_map/jtd,jtr->jdr/dot_general | solution.py:65
  285.5 3.1 %all-to-all-done.1 = bf16[1,4,80,1024]{3,1,0,2:T(4,128)(2,1)S(1)} async-done(((bf16[1,4,80,1024]{3,1,0,2:T(4,128)(2,1)}), bf16[1,4,80,1024]{3,1,0,2:T(4,128)(2,1)S(1)}, u32[]{:S(2)}, u32[]{:S(2)}) %all-to-all-start.1) | async-done | bytes 655392 | tf_op jit(solution)/shard_map/all_to_all | solution.py:48
  288.6 0.3 copy.34
  288.9 0.3 reshape.66
  289.2 1.2 gather_fusion.1
  290.4 12.3 %fusion.4 = bf16[256,1024]{1,0:T(8,128)(2,1)} fusion(bf16[256,8192]{1,0:T(8,128)(2,1)} %param.7, bf16[8192,1024]{1,0:T(8,128)(2,1)} %all-gather.2.cloned.1.call-done, bf16[256,1024]{1,0:T(8,128)(2,1)S(1)} %gather_fusion.1, f32[1024]{0:T(1024)S(1)} %convert_element_type.32), kind=kOutput, calls=%fused_computation.12 | convolution fusion | flops 4296015872 | bytes 22024192 | tf_op jit(solution)/shard_map/dot_general | solution.py:68
  (17 shorter events, 0.2 us)
Async XLA Ops:
  7.2 254.5 %copy-start = (bf16[4,128,1024]{2,1,0:T(8,128)(2,1)S(1)}, bf16[4,128,1024]{2,1,0:T(8,128)(2,1)}, u32[]{:S(2)}) copy-start(bf16[4,128,1024]{2,1,0:T(8,128)(2,1)} %param.13) | copy-start | bytes 3145732
  7.2 283.2 %all-gather.2.cloned.1.call-start = ((), (), s32[]{:S(2)}) async-start(), calls=%async_computation.3 | async-start | bytes 17825792 | tf_op jit(solution)/shard_map/all_gather | solution.py:70
  55.6 7.6 %copy-start.1 = (bf16[256,1024]{1,0:T(8,128)(2,1)S(1)}, bf16[256,1024]{1,0:T(8,128)(2,1)}, u32[]{:S(2)}) copy-start(bf16[256,1024]{1,0:T(8,128)(2,1)} %param.9) | copy-start | bytes 1572868
  55.6 171.3 %all-to-all-start = ((bf16[16,4,5,8192]{3,1,2,0:T(4,128)(2,1)}), bf16[16,4,5,8192]{3,1,2,0:T(4,128)(2,1)}, u32[]{:S(2)}, u32[]{:S(2)}) async-start(bf16[16,4,5,8192]{3,1,2,0:T(4,128)(2,1)} %copy.31), calls=%async_computation | async-start | bytes 10485760 | tf_op jit(solution)/shard_map/all_to_all | solution.py:40
  226.9 40.3 %all-to-all-start.2 = ((bf16[16,4,5,1024]{3,1,2,0:T(4,128)(2,1)}), bf16[16,4,5,1024]{3,1,2,0:T(4,128)(2,1)S(1)}, u32[]{:S(2)}, u32[]{:S(2)}) async-start(bf16[16,4,5,1024]{3,1,2,0:T(4,128)(2,1)} %copy.35), calls=%async_computation.2 | async-start | bytes 1310720 | tf_op jit(solution)/shard_map/all_to_all | solution.py:55
  250.6 21.4 %copy-start.3 = (bf16[1024]{0:T(1024)(128)(2,1)S(1)}, bf16[1024]{0:T(1024)(128)(2,1)}, u32[]{:S(2)}) copy-start(bf16[1024]{0:T(1024)(128)(2,1)} %param.11) | copy-start | bytes 6148
  250.6 21.4 %copy-start.2 = (s32[256,1]{0,1:T(1,128)S(1)}, s32[256,1]{0,1:T(1,128)}, u32[]{:S(2)}) copy-start(s32[256,1]{0,1:T(1,128)} %param.8) | copy-start | bytes 3076
  267.2 21.4 %all-to-all-start.1 = ((bf16[1,4,80,1024]{3,1,0,2:T(4,128)(2,1)}), bf16[1,4,80,1024]{3,1,0,2:T(4,128)(2,1)S(1)}, u32[]{:S(2)}, u32[]{:S(2)}) async-start(bf16[1,4,80,1024]{3,1,0,2:T(4,128)(2,1)} %copy.33), calls=%async_computation.1 | async-start | bytes 1310720 | tf_op jit(solution)/shard_map/all_to_all | solution.py:48
Sparse Core Ops, SparseCore 0:
  10.2 216.6 all-gather.1
where the time goes:
time: 310 us
  waiting for transfers between devices  167 us (54%)
  local copies, waits for them, and re-layouts  43.8 us (14%)
  matrix products  37.1 us (12%)
  starting transfers between devices  36.1 us (12%)
  between operations  14.2 us (5%)
  other arithmetic  11 us (4%)
    all_to_all x1, waiting for transfers between devices, body(): lax.all_to_all(sent_rows, 'fsdp', split_axis=0, concat_axis=2, tiled=True)  160 us
    gather x2, local copies, waits for them, and re-layouts, body(): tokens[source]  25.7 us
    all_to_all x1, starting transfers between devices, body(): lax.all_to_all(sent_grads, 'fsdp', split_axis=0, concat_axis=2, tiled=True)  23.7 us
    dot_general x1, matrix products, body(): jnp.dot(tokens, lax.all_gather(frozen_value_weight, 'fsdp', axis=0, tiled...  12.3 us
    dot_general x1, matrix products, body(): jnp.einsum('jtd,jtr->jdr', local_token_rows, rank_space_gradient, preferr...  11.9 us
    dot_general x1, matrix products, body(): jnp.einsum('ypk,ykv->ypv', local_token_rows, down_factor_weight, preferre...  11.1 us
    select_n x1, local copies, waits for them, and re-layouts, body(): jnp.where(filled[:, None], tokens[source], jnp.zeros((), tokens.dtype))  10.8 us
    select_n x1, other arithmetic, body(): jnp.where(filled[:, None], tokens[source], jnp.zeros((), tokens.dtype))  7.7 us
  transfers between devices with their start and end apart: 4, of which 3 were waited for; matrix products, arithmetic and copies ran while one was open for 26% of the time, Pallas kernels for 0%

commit v1 on v0

--- a/solution.py
+++ b/solution.py
@@ -1,13 +1,23 @@
+import functools
+
 import jax
 import jax.numpy as jnp
 from jax import lax
+from jax.experimental import pallas as pl
+from jax.experimental.pallas import tpu as pltpu
 from jax.sharding import PartitionSpec as P
 
 ADAPTER_JOBS = 64
 JOB_TOKEN_LIMIT = 5
-
-
-def body(
+MESH = pl.DeviceIdType.MESH
+BF16 = jnp.bfloat16
+F32 = jnp.float32
+
+ROWS = 16
+FOLD = 4
+
+
+def plain_body(
     tokens,
     token_job_index,
     cotangent,
@@ -76,7 +86,565 @@
     return (output, down_factor_gradient, up_factor_gradient)
 
 
+def iota(shape, dim):
+    return lax.broadcasted_iota(jnp.int32, shape, dim)
+
+
+def dot(a, b, dims=((1,), (0,)), precision=None):
+    return lax.dot_general(a, b, (dims, ((), ())), precision=precision, preferred_element_type=F32)
+
+
+def exchange_kernel(
+    nz,
+    tok_hbm,
+    job_ref,
+    cot_hbm,
+    w_hbm,
+    bias_ref,
+    d_hbm,
+    u_hbm,
+    out_ref,
+    r_hbm,
+    gl_ref,
+    glx_ref,
+    h_ref,
+    hx_ref,
+    tok,
+    cot,
+    down,
+    up,
+    weight,
+    sent,
+    got,
+    back,
+    returned,
+    pick,
+    pickx,
+    base,
+    hidden,
+    load_sem,
+    a_send,
+    a_recv,
+    b_send,
+    b_recv,
+    zu_send,
+    zu_recv,
+    zd_send,
+    zd_recv,
+    y_send,
+    y_recv,
+    x_send,
+    x_recv,
+    c_send,
+    c_recv,
+):
+    g = lax.axis_index("groups")
+    f = lax.axis_index("fsdp")
+    z, y, c = f // 4, (f // 2) % 2, f % 2
+    count, width = tok.shape
+    value = cot.shape[1]
+    jobs = down.shape[0]
+    rank = down.shape[2]
+    depth = w_hbm.shape[0]
+    half = depth // 2
+    quarter = width // FOLD
+    vquarter = value // FOLD
+    rows = 4 * nz * ROWS
+    v0 = width + quarter
+
+    def place(zz, yy, cc):
+        return zz * 4 + yy * 2 + cc
+
+    offsets = [
+        (oz, oy, oc)
+        for oz in (2, 1, 3, 0)
+        for oy in (1, 0)
+        for oc in (0, 1)
+        if (oz, oy, oc) != (0, 0, 0)
+    ]
+
+    def peer(o, sign):
+        return place((z + sign * o[0] + nz) % nz, (y + o[1]) % 2, (c + o[2]) % 2)
+
+    barrier = pltpu.get_barrier_semaphore()
+    for o in offsets:
+        pl.semaphore_signal(barrier, inc=1, device_id=(g, peer(o, 1)), device_id_type=MESH)
+    pl.semaphore_signal(barrier, inc=1, device_id=(1 - g, f), device_id_type=MESH)
+
+    own_rows = pl.ds(pl.multiple_of(f * depth, depth), depth)
+    loads = [
+        pltpu.make_async_copy(tok_hbm, tok, load_sem.at[0]),
+        pltpu.make_async_copy(cot_hbm, cot, load_sem.at[1]),
+        pltpu.make_async_copy(w_hbm, weight.at[own_rows, :], load_sem.at[2]),
+        pltpu.make_async_copy(d_hbm, down, load_sem.at[3]),
+        pltpu.make_async_copy(u_hbm, up, load_sem.at[4]),
+    ]
+    for load in (loads[2], loads[0], loads[1], loads[3], loads[4]):
+        load.start()
+
+    job = job_ref[...]
+    mine = jnp.where(iota((ADAPTER_JOBS, count), 0) == job, 1.0, 0.0)
+    before = jnp.where(iota((count, count), 0) < iota((count, count), 1), 1.0, 0.0).astype(BF16)
+    earlier = dot(mine.astype(BF16), before)
+    slot = jnp.sum(earlier * mine, axis=0, keepdims=True).astype(jnp.int32)
+    slot = (job % jobs) * JOB_TOKEN_LIMIT + slot
+    first = (job // jobs) * ROWS
+    full = slot < ROWS
+    row = jnp.where(full, first + slot, -rows)
+    rowx = jnp.where(full, -rows, first + slot - ROWS)
+    line = iota((rows, count), 0)
+    pick[...] = jnp.where(line == row, 1.0, 0.0).astype(BF16)
+    for k in range(FOLD):
+        pickx[k] = jnp.where(line == rowx + FOLD * k, 1.0, 0.0).astype(BF16)
+
+    def unit(zz, yy, cc, hh):
+        start = pl.multiple_of(place(zz, yy, cc) * depth + hh * half, half)
+        return weight.at[pl.ds(start, half), :]
+
+    def send_unit(zz, yy, cc, hh, send, recv, device):
+        block = unit(zz, yy, cc, hh)
+        return pltpu.make_async_remote_copy(
+            src_ref=block,
+            dst_ref=block,
+            send_sem=send,
+            recv_sem=recv,
+            device_id=device,
+            device_id_type=MESH,
+        )
+
+    def z_up(k):
+        return send_unit(
+            z - k + 1, y, c, g, zu_send.at[k], zu_recv.at[k], (g, place(z + 1, y, c))
+        )
+
+    def z_up_in(k):
+        return send_unit(z - k, y, c, g, zu_send.at[k], zu_recv.at[k], (g, place(z - 1, y, c)))
+
+    def z_down(k):
+        return send_unit(
+            z + k - 1, y, c, g, zd_send.at[k], zd_recv.at[k], (g, place(z - 1, y, c))
+        )
+
+    def z_down_in(k):
+        return send_unit(z + k, y, c, g, zd_send.at[k], zd_recv.at[k], (g, place(z + 1, y, c)))
+
+    def y_out(zz):
+        return send_unit(zz, y, c, g, y_send.at[zz], y_recv.at[zz], (g, place(z, 1 - y, c)))
+
+    def y_in(zz):
+        return send_unit(zz, 1 - y, c, g, y_send.at[zz], y_recv.at[zz], (g, place(z, 1 - y, c)))
+
+    def x_out(zz, yy):
+        i = zz * 2 + yy
+        return send_unit(zz, yy, c, g, x_send.at[i], x_recv.at[i], (1 - g, f))
+
+    def x_in(zz, yy):
+        i = zz * 2 + yy
+        return send_unit(zz, yy, c, 1 - g, x_send.at[i], x_recv.at[i], (1 - g, f))
+
+    def c_out(zz, yy, hh):
+        i = (zz * 2 + yy) * 2 + hh
+        return send_unit(zz, yy, c, hh, c_send.at[i], c_recv.at[i], (g, place(z, y, 1 - c)))
+
+    def c_in(zz, yy, hh):
+        i = (zz * 2 + yy) * 2 + hh
+        return send_unit(zz, yy, 1 - c, hh, c_send.at[i], c_recv.at[i], (g, place(z, y, 1 - c)))
+
+    pl.semaphore_wait(barrier, len(offsets) + 1)
+    loads[2].wait()
+
+    @pl.when(z < nz - 1)
+    def _():
+        z_up(1).start()
+
+    @pl.when(z > 0)
+    def _():
+        z_down(1).start()
+
+    y_out(z).start()
+    c_out(z, y, g).start()
+    c_out(z, y, 1 - g).start()
+
+    loads[0].wait()
+    loads[1].wait()
+    sent[:, v0 : v0 + value] = dot(pick[...], cot[...]).astype(BF16)
+    folded = jnp.zeros((rows, vquarter), F32)
+    for k in range(FOLD):
+        folded += dot(pickx[k], cot[:, k * vquarter : (k + 1) * vquarter])
+    sent[:, v0 + value :] = folded.astype(BF16)
+    step = quarter // 2
+
+    @pl.loop(0, 2)
+    def _(b):
+        total = jnp.zeros((rows, step), F32)
+        for k in range(FOLD):
+            columns = pl.ds(pl.multiple_of(k * quarter + b * step, step), step)
+            total += dot(pickx[k], tok[:, columns])
+        sent[:, pl.ds(pl.multiple_of(width + b * step, step), step)] = total.astype(BF16)
+
+    @pl.loop(0, width // step)
+    def _(b):
+        columns = pl.ds(pl.multiple_of(b * step, step), step)
+        sent[:, columns] = dot(pick[...], tok[:, columns]).astype(BF16)
+
+    def block(ff):
+        return pl.ds(pl.multiple_of(ff * ROWS, ROWS), ROWS)
+
+    def a_copy(i):
+        there = peer(offsets[i], 1)
+        return pltpu.make_async_remote_copy(
+            src_ref=sent.at[block(there), :],
+            dst_ref=got.at[block(f), :],
+            send_sem=a_send.at[i],
+            recv_sem=a_recv.at[i],
+            device_id=(g, there),
+            device_id_type=MESH,
+        )
+
+    def a_in(i):
+        there = peer(offsets[i], -1)
+        return pltpu.make_async_remote_copy(
+            src_ref=sent.at[block(there), :],
+            dst_ref=got.at[block(there), :],
+            send_sem=a_send.at[i],
+            recv_sem=a_recv.at[i],
+            device_id=(g, there),
+            device_id_type=MESH,
+        )
+
+    for i in range(len(offsets)):
+        a_copy(i).start()
+    got[block(f), :] = sent[block(f), :]
+
+    def after_y(zz):
+        y_in(zz).wait_recv()
+        x_out(zz, 1 - y).start()
+        c_out(zz, 1 - y, g).start()
+
+    def after_z(zz):
+        y_out(zz).start()
+        x_out(zz, y).start()
+        c_out(zz, y, g).start()
+
+    after_y(z)
+    for k in range(1, nz):
+
+        @pl.when(z - k >= 0)
+        def _():
+            z_up_in(k).wait_recv()
+
+            @pl.when(z < nz - 1)
+            def _():
+                z_up(k + 1).start()
+
+            after_z(z - k)
+
+        @pl.when(z + k <= nz - 1)
+        def _():
+            z_down_in(k).wait_recv()
+
+            @pl.when(z > 0)
+            def _():
+                z_down(k + 1).start()
+
+            after_z(z + k)
+
+        @pl.when(z - k >= 0)
+        def _():
+            after_y(z - k)
+
+        @pl.when(z + k <= nz - 1)
+        def _():
+            after_y(z + k)
+
+    def after_x(zz, yy):
+        x_in(zz, yy).wait_recv()
+        c_out(zz, yy, 1 - g).start()
+
+    after_x(z, 1 - y)
+    for k in range(1, nz):
+        for yy in (y, 1 - y):
+
+            @pl.when(z - k >= 0)
+            def _():
+                after_x(z - k, yy)
+
+            @pl.when(z + k <= nz - 1)
+            def _():
+                after_x(z + k, yy)
+
+    for zz in range(nz):
+        for yy in range(2):
+            for hh in range(2):
+                c_in(zz, yy, hh).wait_recv()
+
+    base[...] = jnp.zeros_like(base)
+
+    @pl.loop(0, width // depth)
+    def _(s):
+        along = pl.ds(pl.multiple_of(s * depth, depth), depth)
+        base[...] += dot(tok[:, along], weight[along, :])
+
+    loads[3].wait()
+    loads[4].wait()
+
+    for i in range(len(offsets)):
+        a_in(i).wait_recv()
+    keep = pltpu.make_async_copy(got, r_hbm, load_sem.at[5])
+    keep.start()
+
+    line = iota((rows, jobs * rank), 0) % ROWS
+    lane_job = iota((rows, jobs * rank), 1) // rank
+    of_job = (line >= lane_job * JOB_TOKEN_LIMIT) & (line < (lane_job + 1) * JOB_TOKEN_LIMIT)
+    linex = iota((rows, 1), 0) % ROWS
+    of_quarter = [(linex >= k * FOLD) & (linex < (k + 1) * FOLD) for k in range(FOLD)]
+    ri, ci = iota((rows, rows), 0), iota((rows, rows), 1)
+    same = jnp.where((ri // ROWS == ci // ROWS) & (ri % FOLD == ci % FOLD), 1.0, 0.0)
+
+    hidden[...] = jnp.zeros_like(hidden)
+
+    @pl.loop(0, width // step)
+    def _(b):
+        along = pl.ds(pl.multiple_of(b * step, step), step)
+        factors = jnp.concatenate([down[j, along, :] for j in range(jobs)], axis=1)
+        hidden[...] += dot(got[:, along], factors)
+
+    folds = jnp.zeros((rows, FOLD * rank), F32)
+    for b in range(2):
+        factors = jnp.concatenate(
+            [
+                down[jobs - 1, k * quarter + b * step : k * quarter + (b + 1) * step, :]
+                for k in range(FOLD)
+            ],
+            axis=1,
+        )
+        folds += dot(got[:, width + b * step : width + (b + 1) * step], factors)
+    partial = jnp.zeros((rows, rank), F32)
+    for k in range(FOLD):
+        partial += jnp.where(of_quarter[k], folds[:, k * rank : (k + 1) * rank], 0.0)
+    hx = dot(same, partial, precision=lax.Precision.HIGHEST).astype(BF16)
+    hx_ref[...] = hx
+    h = jnp.where(of_job, hidden[...], 0.0).astype(BF16)
+    h_ref[...] = h
+    back[:, :value] = dot(h, up[...]).astype(BF16)
+    deltax = dot(hx, up[(jobs - 1) * rank :, :])
+    folded = jnp.zeros((rows, vquarter), F32)
+    for k in range(FOLD):
+        folded += jnp.where(of_quarter[k], deltax[:, k * vquarter : (k + 1) * vquarter], 0.0)
+    back[:, value:] = folded.astype(BF16)
+
+    def b_copy(i):
+        there = peer(offsets[i], 1)
+        return pltpu.make_async_remote_copy(
+            src_ref=back.at[block(there), :],
+            dst_ref=returned.at[block(f), :],
+            send_sem=b_send.at[i],
+            recv_sem=b_recv.at[i],
+            device_id=(g, there),
+            device_id_type=MESH,
+        )
+
+    def b_in(i):
+        there = peer(offsets[i], -1)
+        return pltpu.make_async_remote_copy(
+            src_ref=back.at[block(there), :],
+            dst_ref=returned.at[block(there), :],
+            send_sem=b_send.at[i],
+            recv_sem=b_recv.at[i],
+            device_id=(g, there),
+            device_id_type=MESH,
+        )
+
+    for i in range(len(offsets)):
+        b_copy(i).start()
+    returned[block(f), :] = back[block(f), :]
+
+    low = dot(got[:, v0 : v0 + value], up[...], ((1,), (1,)))
+    gl_ref[...] = jnp.where(of_job, low, 0.0).astype(BF16)
+    partial = jnp.zeros((rows, rank), F32)
+    for k in range(FOLD):
+        term = dot(
+            got[:, v0 + value :],
+            up[(jobs - 1) * rank :, k * vquarter : (k + 1) * vquarter],
+            ((1,), (1,)),
+        )
+        partial += jnp.where(of_quarter[k], term, 0.0)
+    glx_ref[...] = dot(same, partial, precision=lax.Precision.HIGHEST).astype(BF16)
+    base[...] += bias_ref[...].astype(F32)
+
+    for i in range(len(offsets)):
+        a_copy(i).wait_send()
+    for k in range(1, nz):
+
+        @pl.when((z < nz - 1) & (z - k + 1 >= 0))
+        def _():
+            z_up(k).wait_send()
+
+        @pl.when((z > 0) & (z + k - 1 <= nz - 1))
+        def _():
+            z_down(k).wait_send()
+
+    for zz in range(nz):
+        y_out(zz).wait_send()
+        x_out(zz, 1 - y).wait_send()
+
+        @pl.when(zz != z)
+        def _():
+            x_out(zz, y).wait_send()
+
+        for yy in range(2):
+            for hh in range(2):
+                c_out(zz, yy, hh).wait_send()
+    keep.wait()
+
+    for i in range(len(offsets)):
+        b_in(i).wait_recv()
+    for k in range(FOLD):
+        columns = slice(k * vquarter, (k + 1) * vquarter)
+        delta = dot(pick[...], returned[:, columns], ((0,), (0,)))
+        delta += dot(pickx[k], returned[:, value:], ((0,), (0,)))
+        out_ref[:, columns] = (base[:, columns] + delta).astype(BF16)
+    for i in range(len(offsets)):
+        b_copy(i).wait_send()
+
+
+def gradient_kernel(per_quarter, r_ref, x_ref, v_ref, gl_ref, glx_ref, h_ref, hx_ref, dg_ref, ug_ref):
+    b = pl.program_id(0)
+    jobs, rank = dg_ref.shape[0], dg_ref.shape[2]
+    value = ug_ref.shape[2]
+    vquarter = value // FOLD
+    rows = r_ref.shape[0]
+    linex = iota((rows, rank), 0) % ROWS // FOLD
+    zero = jnp.zeros((rows, rank), BF16)
+    both = ((0,), (0,))
+    for j in range(jobs):
+        term = dot(r_ref[...], gl_ref[:, j * rank : (j + 1) * rank], both)
+        if j == jobs - 1:
+            glx = jnp.where(linex == b // per_quarter, glx_ref[...], zero)
+            term += dot(x_ref[...], glx, both)
+        dg_ref[j] = term.astype(BF16)
+
+    @pl.when(b == 0)
+    def _():
+        for j in range(jobs):
+            for k in range(FOLD):
+                columns = slice(k * vquarter, (k + 1) * vquarter)
+                term = dot(h_ref[:, j * rank : (j + 1) * rank], v_ref[:, columns], both)
+                if j == jobs - 1:
+                    hx = jnp.where(linex == k, hx_ref[...], zero)
+                    term += dot(hx, v_ref[:, value:], both)
+                ug_ref[j, :, columns] = term.astype(BF16)
+
+
+def fused_body(
+    nz,
+    tokens,
+    token_job_index,
+    cotangent,
+    frozen_value_weight,
+    frozen_value_bias,
+    down_factor_weight,
+    up_factor_weight,
+):
+    count, width = tokens.shape
+    value = cotangent.shape[1]
+    jobs, _, rank = down_factor_weight.shape
+    n = 4 * nz
+    rows = n * ROWS
+    quarter, vquarter = width // FOLD, value // FOLD
+    packed = width + quarter + value + vquarter
+    anywhere = pl.BlockSpec(memory_space=pl.ANY)
+    vmem = pl.BlockSpec(memory_space=pltpu.VMEM)
+    dma = pltpu.SemaphoreType.DMA
+    output, rows_in, gl, glx, h, hx = pl.pallas_call(
+        functools.partial(exchange_kernel, nz),
+        out_shape=(
+            jax.ShapeDtypeStruct((count, value), BF16),
+            jax.ShapeDtypeStruct((rows, packed), BF16),
+            jax.ShapeDtypeStruct((rows, jobs * rank), BF16),
+            jax.ShapeDtypeStruct((rows, rank), BF16),
+            jax.ShapeDtypeStruct((rows, jobs * rank), BF16),
+            jax.ShapeDtypeStruct((rows, rank), BF16),
+        ),
+        in_specs=[anywhere, vmem, anywhere, anywhere, vmem, anywhere, anywhere],
+        out_specs=(vmem, anywhere, vmem, vmem, vmem, vmem),
+        scratch_shapes=[
+            pltpu.VMEM((count, width), BF16),
+            pltpu.VMEM((count, value), BF16),
+            pltpu.VMEM((jobs, width, rank), BF16),
+            pltpu.VMEM((jobs * rank, value), BF16),
+            pltpu.VMEM((width, value), BF16),
+            pltpu.VMEM((rows, packed), BF16),
+            pltpu.VMEM((rows, packed), BF16),
+            pltpu.VMEM((rows, value + vquarter), BF16),
+            pltpu.VMEM((rows, value + vquarter), BF16),
+            pltpu.VMEM((rows, count), BF16),
+            pltpu.VMEM((FOLD, rows, count), BF16),
+            pltpu.VMEM((count, value), F32),
+            pltpu.VMEM((rows, jobs * rank), F32),
+            dma((6,)),
+            dma((n - 1,)),
+            dma((n - 1,)),
+            dma((n - 1,)),
+            dma((n - 1,)),
+            dma((nz + 1,)),
+            dma((nz + 1,)),
+            dma((nz + 1,)),
+            dma((nz + 1,)),
+            dma((nz,)),
+            dma((nz,)),
+            dma((2 * nz,)),
+            dma((2 * nz,)),
+            dma((4 * nz,)),
+            dma((4 * nz,)),
+        ],
+        compiler_params=pltpu.CompilerParams(
+            collective_id=0, has_side_effects=True, vmem_limit_bytes=58 * 1024 * 1024
+        ),
+        name="exchange",
+    )(
+        tokens,
+        token_job_index.reshape(1, count),
+        cotangent,
+        frozen_value_weight,
+        frozen_value_bias.reshape(1, value),
+        down_factor_weight,
+        up_factor_weight.reshape(jobs * rank, value),
+    )
+    step = quarter // 2
+    whole = lambda shape: pl.BlockSpec(shape, lambda b: (0,) * len(shape))
+    down_gradient, up_gradient = pl.pallas_call(
+        functools.partial(gradient_kernel, 2),
+        grid=(width // step,),
+        out_shape=(
+            jax.ShapeDtypeStruct((jobs, width, rank), BF16),
+            jax.ShapeDtypeStruct((jobs, rank, value), BF16),
+        ),
+        in_specs=[
+            pl.BlockSpec((rows, step), lambda b: (0, b)),
+            pl.BlockSpec((rows, step), lambda b: (0, width // step + b % 2)),
+            pl.BlockSpec(
+                (rows, value + vquarter), lambda b: (0, (width + quarter) // (value + vquarter))
+            ),
+            whole((rows, jobs * rank)),
+            whole((rows, rank)),
+            whole((rows, jobs * rank)),
+            whole((rows, rank)),
+        ],
+        out_specs=(
+            pl.BlockSpec((jobs, step, rank), lambda b: (0, b, 0)),
+            whole((jobs, rank, value)),
+        ),
+        compiler_params=pltpu.CompilerParams(vmem_limit_bytes=32 * 1024 * 1024),
+        name="gradients",
+    )(rows_in, rows_in, rows_in, gl, glx, h, hx)
+    return output, down_gradient, up_gradient
+
+
 def solution(mesh):
+    groups, n = mesh.shape["groups"], mesh.shape["fsdp"]
+    fused = groups == 2 and n * 4 == ADAPTER_JOBS
+    body = functools.partial(fused_body, n // 4) if fused else plain_body
     return jax.shard_map(
         body,
         mesh=mesh,

time: 310 us -> 241 us (0.78)
  Pallas kernels: 0 us -> 231 us
  waiting for transfers between devices: 167 us -> 0 us
  matrix products: 37.1 us -> 0 us
  starting transfers between devices: 36.1 us -> 0 us
  local copies, waits for them, and re-layouts: 43.8 us -> 8.32 us
  between operations: 14.2 us -> 0.65 us
  other arithmetic: 11 us -> 0 us
    pallas_call x0 -> x2, Pallas kernels: none -> 231 us  [the longest x1 221 us: fused_body(): pl.pallas_call(functools.partial(exchange_kernel, nz), out_shape=(jax.Sha...]
    all_to_all x3 -> x0, waiting for transfers between devices: 167 us -> none  [the longest x1 160 us: body(): lax.all_to_all(sent_rows, 'fsdp', split_axis=0, concat_axis=2, tiled=True)]
    dot_general x5 -> x0, matrix products: 37.1 us -> none  [the longest x1 12.3 us: body(): jnp.dot(tokens, lax.all_gather(frozen_value_weight, 'fsdp', axis=0, tiled...]
    all_to_all x3 -> x0, starting transfers between devices: 36 us -> none  [the longest x1 23.7 us: body(): lax.all_to_all(sent_grads, 'fsdp', split_axis=0, concat_axis=2, tiled=True)]
    gather x5 -> x0, local copies, waits for them, and re-layouts: 29.3 us -> none  [the longest x2 25.7 us: body(): tokens[source]]
    select_n x2 -> x0, local copies, waits for them, and re-layouts: 12.3 us -> none  [the longest x1 10.8 us: body(): jnp.where(filled[:, None], tokens[source], jnp.zeros((), tokens.dtype))]
    select_n x4 -> x0, other arithmetic: 7.89 us -> none  [the longest x1 7.7 us: body(): jnp.where(filled[:, None], tokens[source], jnp.zeros((), tokens.dtype))]
    unnamed x8 -> x13, local copies, waits for them, and re-layouts: 0.03 us -> 7.04 us
  transfers between devices with their start and end apart: 4 -> 0, of which waited for: 3 -> 0; matrix products, arithmetic and copies ran while one was open for 26% -> 0% of each run, Pallas kernels for 0% -> 0%
where the time goes in v1:
time: 241 us; the launch traced here: 240 us
  Pallas kernels  231 us (96%)
  local copies, waits for them, and re-layouts  8.32 us (3%)
    pallas_call x1, Pallas kernels, fused_body(): pl.pallas_call(functools.partial(exchange_kernel, nz), out_shape=(jax.Sha...  221 us
    pallas_call x1, Pallas kernels, fused_body(): pl.pallas_call(functools.partial(gradient_kernel, 2), grid=(width // step...  10.4 us
    unnamed x13, local copies, waits for them, and re-layouts  7.04 us

profile of v1, /device:TPU:0, one launch (start us, length us, event | category | flops | bytes accessed | tf_op | source)
XLA Modules:
  0.0 240.3 jit_solution(14211372001953998394)
XLA Ops:
  0.6 1.3 reshape.16.bias_ref
  1.9 220.9 %exchange.1 = (bf16[256,1024]{1,0:T(8,128)(2,1)}, bf16[256,11520]{1,0:T(8,128)(2,1)}, bf16[256,512]{1,0:T(8,128)(2,1)}, bf16[256,128]{1,0:T(8,128)(2,1)}, bf16[2...) custom-call(bf16[256,8192]{1,0:T(8,128)(2,1)} %tok_hbm.1, s32[1,256]{1,0:T(1,128)} %bitcast.3, bf16[256,1024]{1,0:T(8,128)(2,1)} %cot_hbm.1, ...), custom_call_target="tpu_custom_call" | custom-call | tf_op jit(solution)/shard_map/exchange/pallas_call | solution.py:559
  222.8 0.0 copy-start
  222.8 2.7 %copy-done = bf16[256,11520]{1,0:T(8,128)(2,1)S(1)} copy-done((bf16[256,11520]{1,0:T(8,128)(2,1)S(1)}, bf16[256,11520]{1,0:T(8,128)(2,1)}, u32[]{:S(2)}) %copy-start) | copy-done | bytes 5898264
  225.5 0.0 copy-start.1
  225.5 0.9 copy-done.1
  226.5 0.0 copy-start.2
  226.5 0.9 copy-done.2
  227.4 0.0 copy-start.3
  227.4 0.8 copy-done.3
  228.2 0.0 copy-start.4
  228.2 0.8 copy-done.4
  229.1 0.0 copy-start.5
  229.1 10.4 %gradients.1 = (bf16[4,8192,128]{2,1,0:T(8,128)(2,1)}, bf16[4,128,1024]{2,1,0:T(8,128)(2,1)}) custom-call(bf16[256,11520]{1,0:T(8,128)(2,1)S(1)} %copy-done, bf16[256,11520]{1,0:T(8,128)(2,1)S(1)} %copy-done, bf16[256,11520]{1,0:T(8,128)(2,1)S(1)} %copy-done, bf16[256,512]{1,0:T(8,128)(2,1)S(1)} %copy-done.1, bf16[256,128]{1,0:T(8,128)(2,1)S(1)} %copy-done.3, ...), custom_call_target="tpu_custom_call" | custom-call | tf_op jit(solution)/shard_map/gradients/pallas_call | solution.py:616
  239.5 0.0 copy-done.5
  239.5 0.8 copy.11
Async XLA Ops:
  222.8 2.7 %copy-start = (bf16[256,11520]{1,0:T(8,128)(2,1)S(1)}, bf16[256,11520]{1,0:T(8,128)(2,1)}, u32[]{:S(2)}) copy-start(bf16[256,11520]{1,0:T(8,128)(2,1)} %get-tuple-element.12.r_ref.x_ref.v_ref) | copy-start | bytes 17694724
  225.5 0.9 copy-start.1
  226.5 0.9 copy-start.2
  227.4 0.8 copy-start.3
  228.2 0.8 copy-start.4
  229.1 10.4 %copy-start.5 = (bf16[256,1024]{1,0:T(8,128)(2,1)S(1)}, bf16[256,1024]{1,0:T(8,128)(2,1)}, u32[]{:S(2)}) copy-start(bf16[256,1024]{1,0:T(8,128)(2,1)} %get-tuple-element.22) | copy-start | bytes 1572868

commit v2 on v1

--- a/solution.py
+++ b/solution.py
@@ -15,6 +15,9 @@
 
 ROWS = 16
 FOLD = 4
+PIECES = 1
+WINDOW = 15
+SPACING = 1
 
 
 def plain_body(
@@ -105,10 +108,7 @@
     u_hbm,
     out_ref,
     r_hbm,
-    gl_ref,
-    glx_ref,
-    h_ref,
-    hx_ref,
+    side_ref,
     tok,
     cot,
     down,
@@ -290,30 +290,35 @@
     def block(ff):
         return pl.ds(pl.multiple_of(ff * ROWS, ROWS), ROWS)
 
-    def a_copy(i):
+    strip = sent.shape[1] // PIECES
+    pieces = [(i, p) for p in range(PIECES) for i in range(len(offsets))]
+
+    def a_copy(q):
+        i, p = pieces[q]
         there = peer(offsets[i], 1)
+        columns = pl.ds(p * strip, strip)
         return pltpu.make_async_remote_copy(
-            src_ref=sent.at[block(there), :],
-            dst_ref=got.at[block(f), :],
-            send_sem=a_send.at[i],
-            recv_sem=a_recv.at[i],
+            src_ref=sent.at[block(there), columns],
+            dst_ref=got.at[block(f), columns],
+            send_sem=a_send.at[q],
+            recv_sem=a_recv.at[q],
             device_id=(g, there),
             device_id_type=MESH,
         )
 
-    def a_in(i):
+    def a_in(q):
+        i, p = pieces[q]
         there = peer(offsets[i], -1)
+        columns = pl.ds(p * strip, strip)
         return pltpu.make_async_remote_copy(
-            src_ref=sent.at[block(there), :],
-            dst_ref=got.at[block(there), :],
-            send_sem=a_send.at[i],
-            recv_sem=a_recv.at[i],
+            src_ref=sent.at[block(there), columns],
+            dst_ref=got.at[block(there), columns],
+            send_sem=a_send.at[q],
+            recv_sem=a_recv.at[q],
             device_id=(g, there),
             device_id_type=MESH,
         )
 
-    for i in range(len(offsets)):
-        a_copy(i).start()
     got[block(f), :] = sent[block(f), :]
 
     def after_y(zz):
@@ -326,9 +331,20 @@
         x_out(zz, y).start()
         c_out(zz, y, g).start()
 
-    after_y(z)
-    for k in range(1, nz):
-
+    def after_x(zz, yy):
+        x_in(zz, yy).wait_recv()
+        c_out(zz, yy, 1 - g).start()
+
+    def either(k, act):
+        @pl.when(z - k >= 0)
+        def _():
+            act(z - k)
+
+        @pl.when(z + k <= nz - 1)
+        def _():
+            act(z + k)
+
+    def relay_z(k):
         @pl.when(z - k >= 0)
         def _():
             z_up_in(k).wait_recv()
@@ -349,47 +365,33 @@
 
             after_z(z + k)
 
-        @pl.when(z - k >= 0)
-        def _():
-            after_y(z - k)
-
-        @pl.when(z + k <= nz - 1)
-        def _():
-            after_y(z + k)
-
-    def after_x(zz, yy):
-        x_in(zz, yy).wait_recv()
-        c_out(zz, yy, 1 - g).start()
-
-    after_x(z, 1 - y)
+    relay_z(1)
+    relays = [lambda: after_y(z)]
     for k in range(1, nz):
-        for yy in (y, 1 - y):
-
-            @pl.when(z - k >= 0)
-            def _():
-                after_x(z - k, yy)
-
-            @pl.when(z + k <= nz - 1)
-            def _():
-                after_x(z + k, yy)
-
-    for zz in range(nz):
-        for yy in range(2):
-            for hh in range(2):
-                c_in(zz, yy, hh).wait_recv()
-
-    base[...] = jnp.zeros_like(base)
-
-    @pl.loop(0, width // depth)
-    def _(s):
-        along = pl.ds(pl.multiple_of(s * depth, depth), depth)
-        base[...] += dot(tok[:, along], weight[along, :])
+        if k > 1:
+            relays.append(functools.partial(relay_z, k))
+        relays.append(functools.partial(either, k, after_y))
+    relays.append(lambda: after_x(z, 1 - y))
+    for k in range(1, nz):
+        relays.append(functools.partial(either, k, lambda zz: after_x(zz, y)))
+        relays.append(functools.partial(either, k, lambda zz: after_x(zz, 1 - y)))
+
+    for q in range(WINDOW):
+        a_copy(q).start()
+    for q in range(len(pieces)):
+        a_copy(q).wait_send()
+        if q + WINDOW < len(pieces):
+            a_copy(q + WINDOW).start()
+        if q % SPACING == SPACING - 1 and relays:
+            relays.pop(0)()
+    for relay in relays:
+        relay()
 
     loads[3].wait()
     loads[4].wait()
 
-    for i in range(len(offsets)):
-        a_in(i).wait_recv()
+    for q in range(len(pieces)):
+        a_in(q).wait_recv()
     keep = pltpu.make_async_copy(got, r_hbm, load_sem.at[5])
     keep.start()
 
@@ -423,9 +425,9 @@
     for k in range(FOLD):
         partial += jnp.where(of_quarter[k], folds[:, k * rank : (k + 1) * rank], 0.0)
     hx = dot(same, partial, precision=lax.Precision.HIGHEST).astype(BF16)
-    hx_ref[...] = hx
+    side_ref[:, 2 * jobs * rank + rank :] = hx
     h = jnp.where(of_job, hidden[...], 0.0).astype(BF16)
-    h_ref[...] = h
+    side_ref[:, jobs * rank : 2 * jobs * rank] = h
     back[:, :value] = dot(h, up[...]).astype(BF16)
     deltax = dot(hx, up[(jobs - 1) * rank :, :])
     folded = jnp.zeros((rows, vquarter), F32)
@@ -460,7 +462,7 @@
     returned[block(f), :] = back[block(f), :]
 
     low = dot(got[:, v0 : v0 + value], up[...], ((1,), (1,)))
-    gl_ref[...] = jnp.where(of_job, low, 0.0).astype(BF16)
+    side_ref[:, : jobs * rank] = jnp.where(of_job, low, 0.0).astype(BF16)
     partial = jnp.zeros((rows, rank), F32)
     for k in range(FOLD):
         term = dot(
@@ -469,11 +471,21 @@
             ((1,), (1,)),
         )
         partial += jnp.where(of_quarter[k], term, 0.0)
-    glx_ref[...] = dot(same, partial, precision=lax.Precision.HIGHEST).astype(BF16)
-    base[...] += bias_ref[...].astype(F32)
-
-    for i in range(len(offsets)):
-        a_copy(i).wait_send()
+    glx = dot(same, partial, precision=lax.Precision.HIGHEST).astype(BF16)
+    side_ref[:, 2 * jobs * rank : 2 * jobs * rank + rank] = glx
+
+    for zz in range(nz):
+        for yy in range(2):
+            for hh in range(2):
+                c_in(zz, yy, hh).wait_recv()
+    base[...] = jnp.zeros_like(base) + bias_ref[...].astype(F32)
+
+    @pl.loop(0, width // depth)
+    def _(s):
+        along = pl.ds(pl.multiple_of(s * depth, depth), depth)
+        base[...] += dot(tok[:, along], weight[along, :])
+
+
     for k in range(1, nz):
 
         @pl.when((z < nz - 1) & (z - k + 1 >= 0))
@@ -508,31 +520,36 @@
         b_copy(i).wait_send()
 
 
-def gradient_kernel(per_quarter, r_ref, x_ref, v_ref, gl_ref, glx_ref, h_ref, hx_ref, dg_ref, ug_ref):
+def gradient_kernel(per_quarter, r_ref, x_ref, v_ref, side_ref, dg_ref, ug_ref):
     b = pl.program_id(0)
     jobs, rank = dg_ref.shape[0], dg_ref.shape[2]
     value = ug_ref.shape[2]
     vquarter = value // FOLD
     rows = r_ref.shape[0]
+    wide = jobs * rank
     linex = iota((rows, rank), 0) % ROWS // FOLD
     zero = jnp.zeros((rows, rank), BF16)
     both = ((0,), (0,))
+    terms = dot(r_ref[...], side_ref[:, :wide], both)
+    glx = jnp.where(linex == b // per_quarter, side_ref[:, 2 * wide : 2 * wide + rank], zero)
+    folded = dot(x_ref[...], glx, both)
     for j in range(jobs):
-        term = dot(r_ref[...], gl_ref[:, j * rank : (j + 1) * rank], both)
+        term = terms[:, j * rank : (j + 1) * rank]
         if j == jobs - 1:
-            glx = jnp.where(linex == b // per_quarter, glx_ref[...], zero)
-            term += dot(x_ref[...], glx, both)
+            term += folded
         dg_ref[j] = term.astype(BF16)
 
     @pl.when(b == 0)
     def _():
-        for j in range(jobs):
-            for k in range(FOLD):
-                columns = slice(k * vquarter, (k + 1) * vquarter)
-                term = dot(h_ref[:, j * rank : (j + 1) * rank], v_ref[:, columns], both)
+        terms = dot(side_ref[:, wide : 2 * wide], v_ref[:, :value], both)
+        for k in range(FOLD):
+            columns = slice(k * vquarter, (k + 1) * vquarter)
+            hx = jnp.where(linex == k, side_ref[:, 2 * wide + rank :], zero)
+            folded = dot(hx, v_ref[:, value:], both)
+            for j in range(jobs):
+                term = terms[j * rank : (j + 1) * rank, columns]
                 if j == jobs - 1:
-                    hx = jnp.where(linex == k, hx_ref[...], zero)
-                    term += dot(hx, v_ref[:, value:], both)
+                    term += folded
                 ug_ref[j, :, columns] = term.astype(BF16)
 
 
@@ -556,18 +573,15 @@
     anywhere = pl.BlockSpec(memory_space=pl.ANY)
     vmem = pl.BlockSpec(memory_space=pltpu.VMEM)
     dma = pltpu.SemaphoreType.DMA
-    output, rows_in, gl, glx, h, hx = pl.pallas_call(
+    output, rows_in, side = pl.pallas_call(
         functools.partial(exchange_kernel, nz),
         out_shape=(
             jax.ShapeDtypeStruct((count, value), BF16),
             jax.ShapeDtypeStruct((rows, packed), BF16),
-            jax.ShapeDtypeStruct((rows, jobs * rank), BF16),
-            jax.ShapeDtypeStruct((rows, rank), BF16),
-            jax.ShapeDtypeStruct((rows, jobs * rank), BF16),
-            jax.ShapeDtypeStruct((rows, rank), BF16),
+            jax.ShapeDtypeStruct((rows, 2 * (jobs + 1) * rank), BF16),
         ),
         in_specs=[anywhere, vmem, anywhere, anywhere, vmem, anywhere, anywhere],
-        out_specs=(vmem, anywhere, vmem, vmem, vmem, vmem),
+        out_specs=(vmem, anywhere, vmem),
         scratch_shapes=[
             pltpu.VMEM((count, width), BF16),
             pltpu.VMEM((count, value), BF16),
@@ -583,8 +597,8 @@
             pltpu.VMEM((count, value), F32),
             pltpu.VMEM((rows, jobs * rank), F32),
             dma((6,)),
-            dma((n - 1,)),
-            dma((n - 1,)),
+            dma((PIECES * (n - 1),)),
+            dma((PIECES * (n - 1),)),
             dma((n - 1,)),
             dma((n - 1,)),
             dma((nz + 1,)),
@@ -626,18 +640,15 @@
             pl.BlockSpec(
                 (rows, value + vquarter), lambda b: (0, (width + quarter) // (value + vquarter))
             ),
-            whole((rows, jobs * rank)),
-            whole((rows, rank)),
-            whole((rows, jobs * rank)),
-            whole((rows, rank)),
+            whole((rows, 2 * (jobs + 1) * rank)),
         ],
         out_specs=(
             pl.BlockSpec((jobs, step, rank), lambda b: (0, b, 0)),
             whole((jobs, rank, value)),
         ),
-        compiler_params=pltpu.CompilerParams(vmem_limit_bytes=32 * 1024 * 1024),
+        compiler_params=pltpu.CompilerParams(vmem_limit_bytes=58 * 1024 * 1024),
         name="gradients",
-    )(rows_in, rows_in, rows_in, gl, glx, h, hx)
+    )(rows_in, rows_in, rows_in, side)
     return output, down_gradient, up_gradient
 
 

time: 241 us -> 198 us (0.82)
  Pallas kernels: 231 us -> 195 us
  local copies, waits for them, and re-layouts: 8.32 us -> 2.08 us
    pallas_call x1, Pallas kernels: 221 us -> 183 us  [fused_body(): pl.pallas_call(functools.partial(exchange_kernel, nz), out_shape=(jax.Sha...]
    unnamed x13 -> x3, local copies, waits for them, and re-layouts: 7.04 us -> 0.8 us
where the time goes in v2:
time: 198 us; the launch traced here: 197 us
  Pallas kernels  195 us (98%)
  local copies, waits for them, and re-layouts  2.08 us (1%)
    pallas_call x1, Pallas kernels, fused_body(): pl.pallas_call(functools.partial(exchange_kernel, nz), out_shape=(jax.Sha...  183 us
    pallas_call x1, Pallas kernels, fused_body(): pl.pallas_call(functools.partial(gradient_kernel, 2), grid=(width // step...  11.7 us

profile of v2, /device:TPU:0, one launch (start us, length us, event | category | flops | bytes accessed | tf_op | source)
XLA Modules:
  0.0 197.3 jit_solution(7508502811554543083)
XLA Ops:
  0.6 1.3 reshape.16.bias_ref
  1.9 182.9 %exchange.1 = (bf16[256,1024]{1,0:T(8,128)(2,1)}, bf16[256,11520]{1,0:T(8,128)(2,1)}, bf16[256,1280]{1,0:T(8,128)(2,1)}) custom-call(bf16[256,8192]{1,0:T(8,128)(2,1)} %tok_hbm.1, s32[1,256]{1,0:T(1,128)} %bitcast.3, bf16[256,1024]{1,0:T(8,128)(2,1)} %cot_hbm.1, bf16[512,1024]{1,0:T(8,128)(2,1)} %w_hbm.1, bf16[1,1024]{1,0:T(2,128)(2,1)} %reshape.16.bias_ref, ...), custom_call_target="tpu_custom_call" | custom-call | tf_op jit(solution)/shard_map/exchange/pallas_call | solution.py:576
  184.8 0.0 copy-start
  184.8 11.7 %gradients.1 = (bf16[4,8192,128]{2,1,0:T(8,128)(2,1)}, bf16[4,128,1024]{2,1,0:T(8,128)(2,1)}) custom-call(bf16[256,11520]{1,0:T(8,128)(2,1)} %get-tuple-element.9.r_ref.x_ref.v_ref, bf16[256,11520]{1,0:T(8,128)(2,1)} %get-tuple-element.9.r_ref.x_ref.v_ref, bf16[256,11520]{1,0:T(8,128)(2,1)} %get-tuple-element.9.r_ref.x_ref.v_ref, ...), custom_call_target="tpu_custom_call" | custom-call | tf_op jit(solution)/shard_map/gradients/pallas_call | solution.py:630
  196.5 0.0 copy-done
  196.5 0.8 copy.11
Async XLA Ops:
  184.8 11.7 %copy-start = (bf16[256,1024]{1,0:T(8,128)(2,1)S(1)}, bf16[256,1024]{1,0:T(8,128)(2,1)}, u32[]{:S(2)}) copy-start(bf16[256,1024]{1,0:T(8,128)(2,1)} %get-tuple-element.16) | copy-start | bytes 1572868

commit v3 on v2

--- a/solution.py
+++ b/solution.py
@@ -520,37 +520,62 @@
         b_copy(i).wait_send()
 
 
-def gradient_kernel(per_quarter, r_ref, x_ref, v_ref, side_ref, dg_ref, ug_ref):
-    b = pl.program_id(0)
-    jobs, rank = dg_ref.shape[0], dg_ref.shape[2]
-    value = ug_ref.shape[2]
+def gradient_kernel(r_hbm, side_ref, dg_hbm, ug_hbm, got, down, up, in_sem, out_sem):
+    jobs, width, rank = down.shape
+    value = up.shape[2]
     vquarter = value // FOLD
-    rows = r_ref.shape[0]
+    rows = got.shape[0]
     wide = jobs * rank
+    quarter = width // FOLD
+    step = quarter // 2
+    blocks = width // step
+    both = ((0,), (0,))
+
+    def load(b):
+        along = slice(b * step, (b + 1) * step) if b < blocks else slice(width, got.shape[1])
+        return pltpu.make_async_copy(r_hbm.at[:, along], got.at[:, along], in_sem.at[b])
+
+    def leave(b, j):
+        along = slice(b * step, (b + 1) * step)
+        return pltpu.make_async_copy(
+            down.at[j, along, :], dg_hbm.at[j, along, :], out_sem.at[b * jobs + j]
+        )
+
+    leave_up = pltpu.make_async_copy(up, ug_hbm, out_sem.at[blocks * jobs])
+    for b in (blocks, *range(blocks)):
+        load(b).start()
     linex = iota((rows, rank), 0) % ROWS // FOLD
     zero = jnp.zeros((rows, rank), BF16)
-    both = ((0,), (0,))
-    terms = dot(r_ref[...], side_ref[:, :wide], both)
-    glx = jnp.where(linex == b // per_quarter, side_ref[:, 2 * wide : 2 * wide + rank], zero)
-    folded = dot(x_ref[...], glx, both)
-    for j in range(jobs):
-        term = terms[:, j * rank : (j + 1) * rank]
-        if j == jobs - 1:
-            term += folded
-        dg_ref[j] = term.astype(BF16)
-
-    @pl.when(b == 0)
-    def _():
-        terms = dot(side_ref[:, wide : 2 * wide], v_ref[:, :value], both)
-        for k in range(FOLD):
-            columns = slice(k * vquarter, (k + 1) * vquarter)
-            hx = jnp.where(linex == k, side_ref[:, 2 * wide + rank :], zero)
-            folded = dot(hx, v_ref[:, value:], both)
-            for j in range(jobs):
-                term = terms[j * rank : (j + 1) * rank, columns]
-                if j == jobs - 1:
-                    term += folded
-                ug_ref[j, :, columns] = term.astype(BF16)
+    load(blocks).wait()
+    for b in range(blocks):
+        load(b).wait()
+        along = slice(b * step, (b + 1) * step)
+        alongx = slice(width + b % 2 * step, width + (b % 2 + 1) * step)
+        terms = dot(got[:, along], side_ref[:, :wide], both)
+        glx = jnp.where(linex == b // 2, side_ref[:, 2 * wide : 2 * wide + rank], zero)
+        folded = dot(got[:, alongx], glx, both)
+        for j in range(jobs):
+            term = terms[:, j * rank : (j + 1) * rank]
+            if j == jobs - 1:
+                term += folded
+            down[j, along, :] = term.astype(BF16)
+            leave(b, j).start()
+    v0 = width + quarter
+    terms = dot(side_ref[:, wide : 2 * wide], got[:, v0 : v0 + value], both)
+    for k in range(FOLD):
+        columns = slice(k * vquarter, (k + 1) * vquarter)
+        hx = jnp.where(linex == k, side_ref[:, 2 * wide + rank :], zero)
+        folded = dot(hx, got[:, v0 + value :], both)
+        for j in range(jobs):
+            term = terms[j * rank : (j + 1) * rank, columns]
+            if j == jobs - 1:
+                term += folded
+            up[j, :, columns] = term.astype(BF16)
+    leave_up.start()
+    for b in range(blocks):
+        for j in range(jobs):
+            leave(b, j).wait()
+    leave_up.wait()
 
 
 def fused_body(
@@ -625,30 +650,24 @@
         down_factor_weight,
         up_factor_weight.reshape(jobs * rank, value),
     )
-    step = quarter // 2
-    whole = lambda shape: pl.BlockSpec(shape, lambda b: (0,) * len(shape))
     down_gradient, up_gradient = pl.pallas_call(
-        functools.partial(gradient_kernel, 2),
-        grid=(width // step,),
+        gradient_kernel,
         out_shape=(
             jax.ShapeDtypeStruct((jobs, width, rank), BF16),
             jax.ShapeDtypeStruct((jobs, rank, value), BF16),
         ),
-        in_specs=[
-            pl.BlockSpec((rows, step), lambda b: (0, b)),
-            pl.BlockSpec((rows, step), lambda b: (0, width // step + b % 2)),
-            pl.BlockSpec(
-                (rows, value + vquarter), lambda b: (0, (width + quarter) // (value + vquarter))
-            ),
-            whole((rows, 2 * (jobs + 1) * rank)),
+        in_specs=[anywhere, vmem],
+        out_specs=(anywhere, anywhere),
+        scratch_shapes=[
+            pltpu.VMEM((rows, packed), BF16),
+            pltpu.VMEM((jobs, width, rank), BF16),
+            pltpu.VMEM((jobs, rank, value), BF16),
+            dma((2 * FOLD + 1,)),
+            dma((2 * FOLD * jobs + 1,)),
         ],
-        out_specs=(
-            pl.BlockSpec((jobs, step, rank), lambda b: (0, b, 0)),
-            whole((jobs, rank, value)),
-        ),
         compiler_params=pltpu.CompilerParams(vmem_limit_bytes=58 * 1024 * 1024),
         name="gradients",
-    )(rows_in, rows_in, rows_in, side)
+    )(rows_in, side)
     return output, down_gradient, up_gradient
 
 

time: 198 us -> 198 us (level)
  Pallas kernels: 195 us -> 193 us
where the time goes in v3:
time: 198 us; the launch traced here: 197 us
  Pallas kernels  193 us (97%)
  local copies, waits for them, and re-layouts  3.15 us (2%)
    pallas_call x1, Pallas kernels, fused_body(): pl.pallas_call(functools.partial(exchange_kernel, nz), out_shape=(jax.Sha...  183 us
    pallas_call x1, Pallas kernels, fused_body(): pl.pallas_call(gradient_kernel, out_shape=(jax.ShapeDtypeStruct((jobs, wi...  10.6 us

profile of v3, /device:TPU:0, one launch (start us, length us, event | category | flops | bytes accessed | tf_op | source)
XLA Modules:
  0.0 197.3 jit_solution(10591716745192359835)
XLA Ops:
  0.6 1.3 reshape.16.bias_ref
  1.9 182.9 %exchange.1 = (bf16[256,1024]{1,0:T(8,128)(2,1)}, bf16[256,11520]{1,0:T(8,128)(2,1)}, bf16[256,1280]{1,0:T(8,128)(2,1)}) custom-call(bf16[256,8192]{1,0:T(8,128)(2,1)} %tok_hbm.1, s32[1,256]{1,0:T(1,128)} %bitcast.3, bf16[256,1024]{1,0:T(8,128)(2,1)} %cot_hbm.1, bf16[512,1024]{1,0:T(8,128)(2,1)} %w_hbm.1, bf16[1,1024]{1,0:T(2,128)(2,1)} %reshape.16.bias_ref, ...), custom_call_target="tpu_custom_call" | custom-call | tf_op jit(solution)/shard_map/exchange/pallas_call | solution.py:601
  184.8 10.6 %gradients.1 = (bf16[4,8192,128]{2,1,0:T(8,128)(2,1)}, bf16[4,128,1024]{2,1,0:T(8,128)(2,1)}) custom-call(bf16[256,11520]{1,0:T(8,128)(2,1)} %get-tuple-element.9.r_hbm, bf16[256,1280]{1,0:T(8,128)(2,1)} %get-tuple-element.10.side_ref), custom_call_target="tpu_custom_call" | custom-call | tf_op jit(solution)/shard_map/gradients/pallas_call | solution.py:653
  195.4 1.9 copy.11
